TPU v7x, 128 devices: a whole 4x4x4 slice. The times are simulated.
128 devices in a mesh: proto: 16 (over x, z), design: 8 (over y, core).
Axes of the slice: x: 4, y: 4, z: 4, core: 2. Of those that a mesh axis runs over, the one named last changes fastest.
Arguments:
- designs: bfloat16 [131072, 1024], P(('proto', 'design')), may hold values from -32 to 32
- prototypes: float32 [32768, 1024], P('proto'), may hold values from -6 to 6
- candidates: int32 [128, 24], P(('proto', 'design')), may hold values from 0 to 255, as said below
- positives: int32 [131072], P(('proto', 'design')), may hold values from 0 to 32767, as said below
Outputs:
- losses: float32 [131072], P(('proto', 'design'))
- design_grad: bfloat16 [131072, 1024], P(('proto', 'design'))
- proto_grad: float32 [32768, 1024], P(('proto', 'design'))
Inputs may be any that keep to these rules, and one draw needn't show every extreme that they name: `candidates`: row g lists 24 distinct blocks for the designs of device g along proto+design. Block b lies in proto shard b // 16; at most 2 blocks of a row lie in one proto shard, and in every draw one shard holds exactly 2 blocks of every row. `positives`: the positive row of design i lies in one of the blocks of row i // 1024 of candidates.
All inputs are finite; a program needn't handle non-finite values.
Results may differ from a plain program's by a relative error of at most 0.0062.
Values may be sent and summed in bfloat16 or wider, within the bound.
A program may use at most 128 MiB of HBM per device.

v0:
```python
import jax
import jax.numpy as jnp
from jax import lax
from jax.sharding import PartitionSpec as P

D = 1024
TILE = 128


def contrast(design_rows, cand_rows, block_list, positive_ids):
    logit_scale = D ** (-0.5)
    logits = (
        lax.dot_general(
            design_rows, cand_rows, (((1,), (1,)), ((), ())), preferred_element_type=jnp.float32
        )
        * logit_scale
    )
    cand_count = block_list.shape[0]
    block_match = (positive_ids // TILE)[:, None] == block_list[None, :]
    cand_index = jnp.sum(
        jnp.where(block_match, jnp.arange(cand_count, dtype=jnp.int32)[None, :], 0), axis=1
    )
    positive_col = cand_index * TILE + positive_ids % TILE
    columns = jnp.arange(cand_count * TILE, dtype=jnp.int32)
    target = columns[None, :] == positive_col[:, None]
    row_max = jnp.max(logits, axis=1, keepdims=True)
    log_total = row_max + jnp.log(jnp.sum(jnp.exp(logits - row_max), axis=1, keepdims=True))
    picked = jnp.sum(jnp.where(target, logits, 0.0), axis=1)
    losses = log_total[:, 0] - picked
    chances = jnp.exp(logits - log_total)
    logit_grad = (chances - target.astype(jnp.float32)).astype(jnp.bfloat16)
    design_grad = jnp.dot(logit_grad, cand_rows, preferred_element_type=jnp.float32).astype(
        jnp.bfloat16
    )
    return (losses, design_grad, logit_grad)


def slot_plan(block_list, blocks_dev, capacity, proto_count):
    owners = block_list // blocks_dev
    local_ids = block_list % blocks_dev
    cand_count = block_list.shape[0]
    cand_ids = jnp.arange(cand_count, dtype=jnp.int32)
    same_owner = owners[:, None] == owners[None, :]
    earlier = cand_ids[None, :] < cand_ids[:, None]
    rank_of = jnp.sum(jnp.where(same_owner & earlier, 1, 0), axis=1).astype(jnp.int32)
    slot_of = owners * capacity + rank_of
    hit_table = slot_of[None, :] == jnp.arange(proto_count * capacity, dtype=jnp.int32)[:, None]
    requested = jnp.sum(jnp.where(hit_table, local_ids[None, :] + 1, 0), axis=1) - 1
    source = jnp.sum(jnp.where(hit_table, cand_ids[None, :], 0), axis=1)
    filled = jnp.any(hit_table, axis=1)
    return (slot_of, requested, source, filled)


def body(designs, prototypes, candidates, positives):
    proto_count = lax.axis_size("proto")
    cand_count = candidates.shape[1]
    blocks_dev = prototypes.shape[0] // TILE
    feature_width = designs.shape[1]
    capacity = max(2, (4 * cand_count + 3 * proto_count - 1) // (3 * proto_count))
    slot_total = proto_count * capacity
    own_list = candidates[0]
    slot_of, requested, source, filled = slot_plan(own_list, blocks_dev, capacity, proto_count)
    incoming = lax.all_to_all(requested, "proto", split_axis=0, concat_axis=0, tiled=True)
    proto_table = prototypes.astype(jnp.bfloat16).reshape(blocks_dev, TILE, feature_width)
    fetched = jnp.take(proto_table, jnp.maximum(incoming, 0), axis=0)
    outgoing = jnp.where((incoming >= 0)[:, None, None], fetched, jnp.zeros((), jnp.bfloat16))
    arrived = lax.all_to_all(outgoing, "proto", split_axis=0, concat_axis=0, tiled=True)
    cand_rows = jnp.take(arrived, slot_of, axis=0).reshape(cand_count * TILE, feature_width)
    losses, design_grad, logit_grad = contrast(designs, cand_rows, own_list, positives)
    tile_grad = lax.dot_general(
        logit_grad, designs, (((0,), (0,)), ((), ())), preferred_element_type=jnp.float32
    )
    tile_grad = tile_grad.reshape(cand_count, TILE, feature_width)
    outgoing_grad = jnp.where(filled[:, None, None], jnp.take(tile_grad, source, axis=0), 0.0)
    returned = lax.all_to_all(outgoing_grad, "proto", split_axis=0, concat_axis=0, tiled=True)
    selector = (incoming[None, :] == jnp.arange(blocks_dev, dtype=jnp.int32)[:, None]).astype(
        jnp.float32
    )
    summed = jnp.dot(
        selector,
        returned.reshape(slot_total, TILE * feature_width),
        precision=lax.Precision.HIGHEST,
        preferred_element_type=jnp.float32,
    )
    summed = summed.reshape(blocks_dev * TILE, feature_width)
    owned_rows = lax.psum_scatter(summed, "design", scatter_dimension=0, tiled=True)
    return (losses, design_grad, owned_rows)


def solution(mesh):
    return jax.shard_map(
        body,
        mesh=mesh,
        in_specs=(
            P(("proto", "design"), None),
            P("proto", None),
            P(("proto", "design"), None),
            P(("proto", "design")),
        ),
        out_specs=(
            P(("proto", "design")),
            P(("proto", "design"), None),
            P(("proto", "design"), None),
        ),
        check_vma=False,
    )
```

profile of v0, /device:TPU:9, one launch (start us, length us, event | category | flops | bytes accessed | tf_op | source)
XLA Modules:
  0.0 517.5 jit_solution(9241015047490938428)
XLA Ops:
  7.2 0.8 and_select_fusion.3
  8.0 0.7 fusion.14
  8.9 0.7 sub.45
  9.6 7.6 %all-to-all-start = ((s32[16,2,1]{1,2,0:T(1,128)}), s32[16,2,1]{1,2,0:T(1,128)S(1)}, u32[]{:S(2)}, u32[]{:S(2)}) async-start(s32[16,2,1]{1,2,0:T(1,128)} %bitcast.6), calls=%async_computation | async-start | bytes 16384 | tf_op jit(solution)/shard_map/all_to_all | solution.py:63
  17.2 6.0 %convert_element_type.13 = bf16[2048,1024]{1,0:T(8,128)(2,1)} convert(f32[2048,1024]{1,0:T(8,128)} %param.5) | non-fusion elementwise | flops 2097152 | bytes 12582912 | tf_op jit(solution)/shard_map/convert_element_type | solution.py:64
  24.1 0.7 fusion.21
  25.0 7.1 %gather_fusion = bf16[32,128,1024]{2,1,0:T(8,128)(2,1)} fusion(bf16[16,128,1024]{2,1,0:T(8,128)(2,1)} %bitcast.68, s32[1024]{0:T(1024)S(1)} %pad_clamp_fusion.2), kind=kCustom, calls=%fused_computation | custom fusion | bytes 16777344 | tf_op jit(solution)/shard_map/jit(_take)/gather | solution.py:65
  32.1 7.6 %select_select_fusion.1 = bf16[32,128,1024]{2,1,0:T(8,128)(2,1)} fusion(bf16[32,128,1024]{2,1,0:T(8,128)(2,1)} %gather_fusion, pred[32]{0:T(512)(128)(4,1)S(1)} %get-tuple-element.12, pred[32]{0:T(512)(128)(4,1)S(1)} %get-tuple-element.11), kind=kLoop, calls=%fused_computation.15 | loop fusion | flops 8388608 | bytes 16777280 | tf_op jit(solution)/shard_map/jit(_where)/select_n | solution.py:66
  39.7 6.3 %all-to-all-start.1 = ((bf16[32,128,1024]{2,1,0:T(8,128)(2,1)}), bf16[32,128,1024]{2,1,0:T(8,128)(2,1)}, u32[]{:S(2)}, u32[]{:S(2)}) async-start(bf16[32,128,1024]{2,1,0:T(8,128)(2,1)} %select_select_fusion.1), calls=%async_computation.1 | async-start | bytes 16777216 | tf_op jit(solution)/shard_map/all_to_all | solution.py:67
  46.7 137.3 %all-to-all-done.1 = bf16[32,128,1024]{2,1,0:T(8,128)(2,1)} async-done(((bf16[32,128,1024]{2,1,0:T(8,128)(2,1)}), bf16[32,128,1024]{2,1,0:T(8,128)(2,1)}, u32[]{:S(2)}, u32[]{:S(2)}) %all-to-all-start.1) | async-done | bytes 8388640 | tf_op jit(solution)/shard_map/all_to_all | solution.py:67
  184.0 7.9 %gather_fusion.1 = bf16[24,128,1024]{2,1,0:T(8,128)(2,1)} fusion(bf16[32,128,1024]{2,1,0:T(8,128)(2,1)} %all-to-all-done.1, s32[1024]{0:T(1024)S(1)} %pad_clamp_fusion.1), kind=kCustom, calls=%fused_computation.1 | custom fusion | bytes 12583008 | tf_op jit(solution)/shard_map/jit(_take)/gather | solution.py:68
  191.8 3.8 bitcast_select_fusion.1
  195.7 7.0 %multiply_reduce_fusion = (f32[1024]{0:T(1024)S(1)}, f32[3072,1024]{1,0:T(8,128)S(1)}) fusion(bf16[3072,1024]{1,0:T(8,128)(2,1)S(1)} %bitcast_select_fusion.1, bf16[1024,1024]{1,0:T(8,128)(2,1)S(1)} %copy-done), kind=kOutput, calls=%fused_computation.14 | convolution fusion | flops 6448741376 | bytes 20975616 | tf_op jit(solution)/shard_map/dot_general | solution.py:13
  202.7 3.6 fusion.2
  206.3 1.1 fusion.22
  207.4 9.3 %fusion.18 = f32[3072,1024]{1,0:T(8,128)} fusion(bf16[1024,1024]{1,0:T(8,128)(2,1)S(1)} %copy-done, f32[3072,1024]{1,0:T(8,128)S(1)} %get-tuple-element.16, f32[1024]{0:T(1024)S(1)} %get-tuple-element.10, s32[1024]{0:T(1024)S(1)} %fusion.9), kind=kOutput, calls=%fused_computation.74 | convolution fusion | flops 6461325312 | bytes 27271168 | tf_op jit(solution)/shard_map/dot_general | solution.py:70
  216.7 12.9 %gather_fusion.2 = f32[32,128,1024]{2,1,0:T(8,128)} fusion(f32[24,128,1024]{2,1,0:T(8,128)} %bitcast.69, s32[1024]{0:T(1024)S(1)} %pad_clamp_fusion), kind=kCustom, calls=%fused_computation.2 | custom fusion | bytes 33554560 | tf_op jit(solution)/shard_map/jit(_take)/gather | solution.py:74
  229.6 7.2 %select_select_fusion = f32[32,128,1024]{2,1,0:T(8,128)S(1)} fusion(f32[32,128,1024]{2,1,0:T(8,128)} %gather_fusion.2, pred[32]{0:T(512)(128)(4,1)S(1)} %compare_and_fusion, pred[32]{0:T(512)(128)(4,1)S(1)} %fusion.6), kind=kLoop, calls=%fused_computation.3 | loop fusion | flops 8388608 | bytes 33554496 | tf_op jit(solution)/shard_map/jit(_where)/select_n | solution.py:74
  236.8 189.1 %all_to_all.19 = f32[32,128,1024]{2,1,0:T(8,128)} all-to-all(f32[32,128,1024]{2,1,0:T(8,128)S(1)} %select_select_fusion), channel_id=1, replica_groups=mesh['proto'=16,'design'=8] {'proto'}, dimensions={0} | all-to-all | bytes 33554432 | tf_op jit(solution)/shard_map/all_to_all | solution.py:75
  425.9 15.2 %copy.9 = f32[4,8,128,1024]{3,1,2,0:T(8,128)S(1)} copy(f32[4,8,128,1024]{3,2,1,0:T(8,128)} %bitcast.67) | data formatting | bytes 33554432
  441.1 8.1 %fusion.8 = f32[16,131072]{1,0:T(8,128)} fusion(f32[32,131072]{1,0:T(8,128)S(1)} %bitcast.66, s32[32]{0:T(128)S(1)} %all_to_all.13), kind=kOutput, calls=%fused_computation.28 | convolution fusion | flops 805306880 | bytes 25165952 | tf_op jit(solution)/shard_map/dot_general | solution.py:79
  449.2 6.2 %reshape.200 = f32[2048,1024]{1,0:T(8,128)} reshape(f32[16,131072]{1,0:T(8,128)} %fusion.8) | data formatting | bytes 16777216 | tf_op jit(solution)/shard_map/reshape | solution.py:85
  455.4 13.7 %convolution_convert_fusion = bf16[1024,1024]{1,0:T(8,128)(2,1)} fusion(bf16[3072,1024]{1,0:T(8,128)(2,1)} %copy-done.3, f32[3072,1024]{1,0:T(8,128)} %copy-done.2, f32[1024]{0:T(1024)S(1)} %get-tuple-element.10, s32[1024]{0:T(1024)S(1)} %fusion.9), kind=kOutput, calls=%fused_computation.17 | convolution fusion | flops 6462373888 | bytes 20979712 | tf_op jit(solution)/shard_map/dot_general | solution.py:32
  469.1 41.6 %reduce-scatter.2.cloned.1.call-done = f32[256,1024]{1,0:T(8,128)} async-done(((f32[2048,1024]{1,0:T(8,128)}), f32[256,1024]{1,0:T(8,128)}) %reduce-scatter.2.cloned.1.call-update) | async-done | bytes 1048592 | tf_op jit(solution)/shard_map/reduce_scatter | solution.py:86
  (35 shorter events, 1.9 us)
Async XLA Ops:
  7.2 188.5 %copy-start = (bf16[1024,1024]{1,0:T(8,128)(2,1)S(1)}, bf16[1024,1024]{1,0:T(8,128)(2,1)}, u32[]{:S(2)}) copy-start(bf16[1024,1024]{1,0:T(8,128)(2,1)} %param.4) | copy-start | bytes 6291460
  9.6 13.9 %all-to-all-start = ((s32[16,2,1]{1,2,0:T(1,128)}), s32[16,2,1]{1,2,0:T(1,128)S(1)}, u32[]{:S(2)}, u32[]{:S(2)}) async-start(s32[16,2,1]{1,2,0:T(1,128)} %bitcast.6), calls=%async_computation | async-start | bytes 16384 | tf_op jit(solution)/shard_map/all_to_all | solution.py:63
  39.7 6.6 %copy-start.5 = (s32[1,24]{1,0:T(1,128)S(1)}, s32[1,24]{1,0:T(1,128)}, u32[]{:S(2)}) copy-start(s32[1,24]{1,0:T(1,128)} %param.6) | copy-start | bytes 292
  39.7 6.7 %copy-start.4 = (s32[1024]{0:T(1024)S(1)}, s32[1024]{0:T(1024)}, u32[]{:S(2)}) copy-start(s32[1024]{0:T(1024)} %param.7) | copy-start | bytes 12292
  39.7 144.2 %all-to-all-start.1 = ((bf16[32,128,1024]{2,1,0:T(8,128)(2,1)}), bf16[32,128,1024]{2,1,0:T(8,128)(2,1)}, u32[]{:S(2)}, u32[]{:S(2)}) async-start(bf16[32,128,1024]{2,1,0:T(8,128)(2,1)} %select_select_fusion.1), calls=%async_computation.1 | async-start | bytes 16777216 | tf_op jit(solution)/shard_map/all_to_all | solution.py:67
  46.0 464.6 %reduce-scatter.2.cloned.1.call-start = ((), (), s32[]{:S(2)}) async-start(), calls=%async_computation.4 | async-start | bytes 9437184 | tf_op jit(solution)/shard_map/reduce_scatter | solution.py:86
  195.7 7.0 %copy-start.3 = (bf16[3072,1024]{1,0:T(8,128)(2,1)}, bf16[3072,1024]{1,0:T(8,128)(2,1)S(1)}, u32[]{:S(2)}) copy-start(bf16[3072,1024]{1,0:T(8,128)(2,1)S(1)} %bitcast_select_fusion.1) | copy-start | bytes 18874372
  202.7 14.1 %copy-start.2 = (f32[3072,1024]{1,0:T(8,128)}, f32[3072,1024]{1,0:T(8,128)S(1)}, u32[]{:S(2)}) copy-start(f32[3072,1024]{1,0:T(8,128)S(1)} %get-tuple-element.16) | copy-start | bytes 37748740
  455.4 55.3 %copy-start.1 = (bf16[1024,1024]{1,0:T(8,128)(2,1)S(1)}, bf16[1024,1024]{1,0:T(8,128)(2,1)}, u32[]{:S(2)}) copy-start(bf16[1024,1024]{1,0:T(8,128)(2,1)} %param.4) | copy-start | bytes 6291460
Sparse Core Ops, SparseCore 0:
  455.5 55.1 reduce-scatter.1
where the time goes:
time: 521 us; the launch traced here: 518 us
  blocking collectives  189 us (36%)
  waiting for transfers between devices  179 us (34%)
  local copies, waits for them, and re-layouts  50.7 us (10%)
  matrix products  38.1 us (7%)
  other arithmetic  32 us (6%)
  between operations  14.2 us (3%)
  starting transfers between devices  14.1 us (3%)
    all_to_all x1, blocking collectives, body(): lax.all_to_all(outgoing_grad, 'proto', split_axis=0, concat_axis=0, tiled...  189 us
    all_to_all x1, waiting for transfers between devices, body(): lax.all_to_all(outgoing, 'proto', split_axis=0, concat_axis=0, tiled=True)  137 us
    reduce_scatter x1, waiting for transfers between devices, body(): lax.psum_scatter(summed, 'design', scatter_dimension=0, tiled=True)  41.6 us
    unnamed x13, local copies, waits for them, and re-layouts  15.2 us
    dot_general x1, matrix products, contrast(): jnp.dot(logit_grad, cand_rows, preferred_element_type=jnp.float32)  13.7 us
    gather x1, local copies, waits for them, and re-layouts, body(): jnp.take(tile_grad, source, axis=0)  12.9 us
  transfers between devices with their start and end apart: 3, of which 3 were waited for; matrix products, arithmetic and copies ran while one was open for 4% of the time, Pallas kernels for 0%

commit v1 on v0

v1 whole, which is shorter than its diff:
```python
import jax
import jax.numpy as jnp
from jax import lax
from jax.experimental import pallas as pl
from jax.experimental.pallas import tpu as pltpu
from jax.sharding import PartitionSpec as P

D = 1024
HALF = 512
TILE = 128
ROWS = 1024
SIDE = 4
BLOCKS = 16
CANDS = 24
PAIR = 2 * TILE
COLS = 256
LOW = -3.0e38
MESH = pl.DeviceIdType.MESH
BF16 = jnp.bfloat16
F32 = jnp.float32
I32 = jnp.int32


def remote(src, dst, send_sem, recv_sem, device):
    return pltpu.make_async_remote_copy(
        src_ref=src, dst_ref=dst, send_sem=send_sem, recv_sem=recv_sem, device_id=device, device_id_type=MESH
    )


def iota(shape, dim):
    return lax.broadcasted_iota(I32, shape, dim)


def to_column(row):
    n = row.shape[1]
    return jnp.sum(jnp.where(iota((n, n), 0) == iota((n, n), 1), jnp.broadcast_to(row, (n, n)), 0), axis=1, keepdims=True)


def to_row(col):
    n = col.shape[0]
    return jnp.sum(jnp.where(iota((n, n), 0) == iota((n, n), 1), jnp.broadcast_to(col, (n, n)), 0), axis=0, keepdims=True)


def gray(k):
    return k + (k // 2) * (1 - 2 * (k % 2))


def pair_of(n):
    s = jnp.where(n >= 1, 1, 0) + jnp.where(n >= 4, 1, 0) + jnp.where(n >= 9, 1, 0)
    m = n - s * s
    return gray(jnp.minimum(s, 2 * s - m)), gray(jnp.minimum(m, s))


def kernel(
    des, proto, cand, pos, loss_o, dg_o, pg_o,
    tab0, tab1, tab2, tab3, rr0, rr1, rr2, rr3,
    send, arr_m, arr_o, des_m, des_o, dt_m, dt_o, grads, stage, merge, from_up, from_down, from_y, runs, core_in, dg_s,
    prow, m_run, s_run, pick, total, req_v, req_in, order_v, req_own, req_s, order_s,
    ld_sem, des_sem, out_sem, loc_sem, own_sem, rq_s, rq_r, ag_s, ag_r, rl_s, rl_r, f_s, fm_r, fo_r, b_s, b_r,
    mg_s, mg_r, rs_s, rs_r, y_s, y_r, c_s, c_r,
):
    p, d = lax.axis_index("proto"), lax.axis_index("design")
    x, z, y, r = p // SIDE, p % SIDE, d // 2, d % 2
    tab, rr = (tab0, tab1, tab2, tab3), (rr0, rr1, rr2, rr3)

    def owner(ku, kv):
        return ((x + ku * (1 - r) + kv * r) % SIDE) * SIDE + (z + ku * r + kv * (1 - r)) % SIDE

    def along_u(k, core):
        return (owner(k, 0), y * 2 + core)

    def along_v(k, core):
        return (owner(0, k), y * 2 + core)

    sibling = (p, y * 2 + 1 - r)
    my_cols = pl.ds(pl.multiple_of(r * HALF, HALF), HALF)
    other_cols = pl.ds(pl.multiple_of((1 - r) * HALF, HALF), HALF)

    def load(k):
        return pltpu.make_async_copy(proto.at[pl.ds(k * HALF, HALF), my_cols], stage.at[k % 2], ld_sem.at[k])

    load(0).start()
    load(1).start()
    designs_in = [
        pltpu.make_async_copy(des.at[:, my_cols], des_m, des_sem.at[0]),
        pltpu.make_async_copy(des.at[:, other_cols], des_o, des_sem.at[1]),
    ]
    for c in designs_in:
        c.start()

    barrier = pltpu.get_barrier_semaphore()
    partners = [sibling]
    for k in (1, 2, 3):
        partners += [along_v(k, r), along_v(k, 1 - r), along_u(k, 1 - r), (p, ((y + k) % SIDE) * 2 + r)]
    partners += [along_u(1, r), along_u(3, r)]
    for q in partners:
        pl.semaphore_signal(barrier, inc=1, device_id=q, device_id_type=MESH)

    row = cand[...]
    col = to_column(row)
    same = (row >> 4) == (col >> 4)
    rank = jnp.sum(jnp.where(same & (iota((CANDS, CANDS), 1) < iota((CANDS, CANDS), 0)), 1, 0), axis=1, keepdims=True)
    slot = (col >> 4) * 2 + rank
    hit = slot == iota((CANDS, TILE), 1)
    wanted = jnp.sum(jnp.where(hit, (col & 15) + 1, 0), axis=0, keepdims=True) - 1
    req_v[...] = jnp.broadcast_to(wanted, (8, TILE))
    block = pos[...] >> 7
    spot = jnp.sum(jnp.where(col == block, slot, 0), axis=0, keepdims=True)
    prow[...] = spot * TILE + (pos[...] & 127)
    pltpu.make_async_copy(req_v, req_own, own_sem).start()

    pl.semaphore_wait(barrier, len(partners))

    req_in[0] = req_v[...]
    requests = [remote(req_v, req_in.at[1], rq_s.at[0], rq_r.at[1], sibling)]
    for k in (1, 2, 3):
        back = (SIDE - k) * 2
        requests.append(remote(req_v, req_in.at[back], rq_s.at[2 * k - 1], rq_r.at[back], along_v(k, r)))
        requests.append(remote(req_v, req_in.at[back + 1], rq_s.at[2 * k], rq_r.at[back + 1], along_u(k, 1 - r)))
    for c in requests:
        c.start()

    def own_chunk(k, way):
        part = pl.ds(4 * k, 4)
        dst = tab3 if way == 0 else tab1
        return remote(tab0.at[part], dst.at[part], ag_s.at[way, k], ag_r.at[way, k], along_u(1 if way == 0 else 3, r))

    for k in range(4):
        load(k).wait()
        for b in range(4):
            tab0[4 * k + b] = stage[k % 2, TILE * b : TILE * (b + 1)].astype(BF16)
        own_chunk(k, 0).start()
        own_chunk(k, 1).start()
        if k < 2:
            load(k + 2).start()

    for c in designs_in:
        c.wait()

    @pl.loop(0, 4)
    def _(i):
        part = pl.ds(pl.multiple_of(i * COLS, COLS), COLS)
        dt_m[:, part] = des_m[part, :].T
        dt_o[:, part] = des_o[part, :].T

    for n in range(1, 8):
        remote(req_v, req_in.at[n], rq_s.at[0], rq_r.at[n], sibling).wait_recv()
    to_scalars = pltpu.make_async_copy(req_in, req_s, loc_sem.at[0])
    to_scalars.start()
    to_scalars.wait()

    def wanted_blocks(ku):
        first = owner(ku, 0) * 2
        for n in range(8):
            k, so = n // 2, n % 2
            for i in range(2):
                val = tab[ku][jnp.maximum(req_s[n, 0, first + i], 0)]
                if n == 0:
                    arr_m[0, ku, i] = val
                else:
                    send[n, ku, i] = val
            if n:
                fetched(n, ku).start()

    def fetched(n, ku):
        k, so = n // 2, n % 2
        back = (SIDE - k) % SIDE
        if so == 0:
            return remote(send.at[n, ku], arr_m.at[back, ku], f_s.at[n, ku], fm_r.at[back, ku], along_v(k, r))
        return remote(send.at[n, ku], arr_o.at[back, ku], f_s.at[n, ku], fo_r.at[back, ku], along_v(k, 1 - r))

    def relay(k):
        part = pl.ds(4 * k, 4)
        src, to = (tab3, 1) if k < 2 else (tab1, 3)
        return remote(src.at[part], tab2.at[part], rl_s.at[k], rl_r.at[k], along_u(to, r))

    def pass_on(k):
        own_chunk(k, 0 if k < 2 else 1).wait_recv()
        relay(k).start()

    pass_on(0)
    wanted_blocks(0)
    pass_on(1)
    own_chunk(0, 1).wait_recv()
    own_chunk(1, 1).wait_recv()
    pass_on(2)
    own_chunk(2, 0).wait_recv()
    pass_on(3)
    own_chunk(3, 0).wait_recv()
    wanted_blocks(1)
    wanted_blocks(3)
    for k in range(4):
        relay(k).wait_recv()
    wanted_blocks(2)

    for ku in range(4):
        first = owner(ku, 0) * 2
        eye = iota((8, TILE), 1)
        reqs = req_in[:, 0, :]
        ids = [jnp.sum(jnp.where(eye == first + i, reqs, 0), axis=1, keepdims=True) for i in range(2)]
        ids = jnp.concatenate(ids, axis=0)
        place = iota((BLOCKS, 1), 0)
        entry = (place % 8) * 2 + place // 8
        key = ids * BLOCKS + entry
        rank = jnp.sum(jnp.where(to_row(key) < key, 1, 0), axis=1, keepdims=True)
        at = rank == iota((BLOCKS, TILE), 1)
        follows = jnp.sum(jnp.where((to_row(key) < key) & (to_row(ids) == ids), 1, 0), axis=1, keepdims=True)
        lane = iota((BLOCKS, TILE), 1)
        rows = [
            jnp.sum(jnp.where(at, entry, 0), axis=0, keepdims=True),
            jnp.sum(jnp.where(at & (follows == 0), 1, 0), axis=0, keepdims=True),
            jnp.maximum(jnp.sum(jnp.where(ids <= lane, 1, 0), axis=0, keepdims=True) - 1, 0),
            jnp.sum(jnp.where(ids == lane, 1, 0), axis=0, keepdims=True),
        ]
        for i in range(4):
            order_v[ku, i : i + 1, :] = rows[i]
    order_copy = pltpu.make_async_copy(order_v, order_s, loc_sem.at[1])
    order_copy.start()
    pltpu.make_async_copy(req_v, req_own, own_sem).wait()

    def logits_of(ku, kv, part):
        o = owner(ku, kv)
        left = jnp.dot(arr_m[kv, ku].reshape(PAIR, HALF), dt_m[:, part], preferred_element_type=F32)
        right = jnp.dot(arr_o[ku, kv].reshape(PAIR, HALF), dt_o[:, part], preferred_element_type=F32)
        rows = iota((PAIR, COLS), 0)
        held = jnp.where(rows < TILE, req_own[0, o * 2], req_own[0, o * 2 + 1]) >= 0
        target = rows + o * PAIR == prow[:, part]
        return jnp.where(held, (left + right) * D**-0.5, LOW), target

    m_run[...] = jnp.full((1, ROWS), LOW, F32)
    s_run[...] = jnp.zeros((1, ROWS), F32)
    pick[...] = jnp.zeros((1, ROWS), F32)

    @pl.loop(0, 16)
    def _(n):
        ku, kv = pair_of(n)

        @pl.when(kv != 0)
        def _():
            remote(send.at[1, 0], arr_m.at[kv, ku], f_s.at[1, 0], fm_r.at[kv, ku], sibling).wait_recv()

        remote(send.at[1, 0], arr_o.at[ku, kv], f_s.at[1, 0], fo_r.at[ku, kv], sibling).wait_recv()

        @pl.loop(0, ROWS // COLS)
        def _(i):
            part = pl.ds(pl.multiple_of(i * COLS, COLS), COLS)
            logits, target = logits_of(ku, kv, part)
            pick[:, part] += jnp.sum(jnp.where(target, logits, 0.0), axis=0, keepdims=True)
            before = m_run[:, part]
            now = jnp.maximum(before, jnp.max(logits, axis=0, keepdims=True))
            m_run[:, part] = now
            s_run[:, part] = s_run[:, part] * jnp.exp(before - now) + jnp.sum(jnp.exp(logits - now), axis=0, keepdims=True)

    total[...] = m_run[...] + jnp.log(s_run[...])
    loss_o[...] = total[...] - pick[...]

    for n in range(1, 8):
        for ku in range(4):
            fetched(n, ku).wait_send()
    for c in requests:
        c.wait_send()
    for k in range(4):
        own_chunk(k, 0).wait_send()
        own_chunk(k, 1).wait_send()
        relay(k).wait_send()

    def back_mine(ku, kv, k):
        back = (SIDE - kv) % SIDE
        return remote(send.at[kv * 2, ku], rr[k].at[pl.ds(back * 4, 2)], b_s.at[kv * 2, ku], b_r.at[k, back, 0], along_v(kv, r))

    def back_other(ku, kv, k):
        back = (SIDE - ku) % SIDE
        return remote(send.at[ku * 2 + 1, kv], rr[k].at[pl.ds(back * 4 + 2, 2)], b_s.at[ku * 2 + 1, kv], b_r.at[k, back, 1], along_u(ku, 1 - r))

    @pl.loop(0, 16)
    def _(n):
        ku, kv = pair_of(15 - n)

        @pl.loop(0, ROWS // COLS)
        def _(i):
            part = pl.ds(pl.multiple_of(i * COLS, COLS), COLS)
            logits, target = logits_of(ku, kv, part)
            grads[kv, ku, :, part] = (jnp.exp(logits - total[:, part]) - jnp.where(target, 1.0, 0.0)).astype(BF16)

        mine = jnp.dot(grads[kv, ku], des_m[...], preferred_element_type=F32).astype(BF16).reshape(2, TILE, HALF)
        send[kv * 2, ku] = mine
        other = jnp.dot(grads[kv, ku], des_o[...], preferred_element_type=F32).astype(BF16).reshape(2, TILE, HALF)
        send[ku * 2 + 1, kv] = other
        for k in range(4):

            @pl.when(ku == k)
            def _():
                @pl.when(kv == 0)
                def _():
                    rr[k][0:2] = send[0, k]

                @pl.when(kv != 0)
                def _():
                    back_mine(ku, kv, k).start()

            @pl.when(kv == k)
            def _():
                back_other(ku, kv, k).start()

    order_copy.wait()

    def sums(ku):
        for n in range(1, 8):
            k, so = n // 2, n % 2
            remote(send.at[1, 0], rr[ku].at[pl.ds(2 * n, 2)], b_s.at[1, 0], b_r.at[ku, k, so], sibling).wait_recv()

        @pl.loop(0, TILE // 16)
        def _(i):
            part = pl.ds(pl.multiple_of(i * 16, 16), 16)
            acc = jnp.zeros((16, HALF), F32)
            for t in range(BLOCKS):
                val = rr[ku][order_s[ku, 0, t], part, :].astype(F32)
                acc = jnp.where(order_s[ku, 1, t] == 1, val, acc + val)
                runs[t] = acc
            for j in range(BLOCKS):
                val = runs[order_s[ku, 2, j]]
                tab[ku][j, part, :] = jnp.where(order_s[ku, 3, j] > 0, val, 0.0).astype(BF16)

    def design_grad(q):
        part = pl.ds(q * COLS, COLS)
        for h in range(2):
            acc = stage.at[0, pl.ds(0, COLS)]
            acc[...] = jnp.zeros((COLS, HALF), F32)

            @pl.loop(0, 4)
            def _(k):
                lhs = grads[k, :, :, part] if h == 0 else grads[:, k, :, part]
                rhs = arr_m[k] if h == 0 else arr_o[k]
                acc[...] += lax.dot_general(
                    lhs.reshape(ROWS, COLS), rhs.reshape(ROWS, HALF), (((0,), (0,)), ((), ())), preferred_element_type=F32
                )

            dg_s[q, h] = acc[...].astype(BF16)
            dg_out(q, h).start()

    def dg_out(q, h):
        cols = my_cols if h == 0 else other_cols
        return pltpu.make_async_copy(dg_s.at[q, h], dg_o.at[pl.ds(q * COLS, COLS), cols], out_sem.at[q, h])

    def far(g):
        part = pl.ds(4 * g, 4)
        return remote(tab2.at[part], merge.at[g], mg_s.at[g], mg_r.at[g], along_u(1 if g < 2 else 3, r))

    def near(g, way):
        part = pl.ds(4 * g, 4)
        if way == 0:
            return remote(tab1.at[part], from_down.at[g], rs_s.at[0, g], rs_r.at[0, g], along_u(1, r))
        return remote(tab3.at[part], from_up.at[g], rs_s.at[1, g], rs_r.at[1, g], along_u(3, r))

    def merged(g):
        src = tab1 if g < 2 else tab3
        far(g).wait_recv()
        for b in range(4):
            src[4 * g + b] = (src[4 * g + b].astype(F32) + merge[g, b].astype(F32)).astype(BF16)
        near(g, 0 if g < 2 else 1).start()

    sums(2)
    for g in (0, 2, 1, 3):
        far(g).start()
    design_grad(0)
    sums(1)
    near(2, 0).start()
    near(3, 0).start()
    sums(3)
    near(0, 1).start()
    near(1, 1).start()
    for g in (0, 2, 1, 3):
        merged(g)
    sums(0)
    design_grad(1)
    design_grad(2)

    def to_y(g):
        return remote(tab0.at[pl.ds(4 * g, 4)], from_y.at[(y - g + SIDE) % SIDE], y_s.at[g], y_r.at[(y - g + SIDE) % SIDE], (p, g * 2 + r))

    for g in (0, 2, 1, 3):
        near(g, 0).wait_recv()
        near(g, 1).wait_recv()
        for b in range(4):
            val = tab0[4 * g + b].astype(F32) + from_up[g, b].astype(F32) + from_down[g, b].astype(F32)
            tab0[4 * g + b] = val.astype(BF16)

        @pl.when(y != g)
        def _():
            to_y(g).start()

    design_grad(3)
    for k in (1, 3, 2):
        remote(tab0.at[pl.ds(0, 4)], from_y.at[k], y_s.at[0], y_r.at[k], sibling).wait_recv()

    def reduced(b):
        val = tab0[4 * y + b].astype(F32)
        for k in (1, 2, 3):
            val += from_y[k, b].astype(F32)
        return val

    for i in range(2):
        stage[1, pl.ds(PAIR + i * TILE, TILE)] = reduced(2 * (1 - r) + i)
    cross = remote(stage.at[1, pl.ds(PAIR, PAIR)], core_in, c_s, c_r, sibling)
    cross.start()
    for i in range(2):
        stage[1, pl.ds(i * TILE, TILE)] = reduced(2 * r + i)
    outs = [pltpu.make_async_copy(stage.at[1, pl.ds(0, PAIR)], pg_o.at[:, my_cols], loc_sem.at[2])]
    outs[0].start()
    cross.wait_recv()
    outs.append(pltpu.make_async_copy(core_in, pg_o.at[:, other_cols], loc_sem.at[3]))
    outs[1].start()

    for kv in range(4):
        for ku in range(4):
            if kv:
                back_mine(ku, kv, ku).wait_send()
            back_other(ku, kv, kv).wait_send()
    for g in range(4):
        far(g).wait_send()
        near(g, 0).wait_send()
        near(g, 1).wait_send()

        @pl.when(y != g)
        def _():
            to_y(g).wait_send()

        for h in range(2):
            dg_out(g, h).wait()
    cross.wait_send()
    for c in outs:
        c.wait()


def body(designs, prototypes, candidates, positives):
    vmem = lambda shape, dtype: pltpu.VMEM(shape, dtype)
    dma = lambda *shape: pltpu.SemaphoreType.DMA(shape)
    blocks = (BLOCKS, TILE, HALF)
    pairs = (SIDE, SIDE, 2, TILE, HALF)
    losses, design_grad, proto_grad = pl.pallas_call(
        kernel,
        out_shape=(
            jax.ShapeDtypeStruct((1, ROWS), F32),
            jax.ShapeDtypeStruct((ROWS, D), BF16),
            jax.ShapeDtypeStruct((PAIR, D), F32),
        ),
        in_specs=[
            pl.BlockSpec(memory_space=pl.ANY),
            pl.BlockSpec(memory_space=pl.ANY),
            pl.BlockSpec(memory_space=pltpu.VMEM),
            pl.BlockSpec(memory_space=pltpu.VMEM),
        ],
        out_specs=(
            pl.BlockSpec(memory_space=pltpu.VMEM),
            pl.BlockSpec(memory_space=pl.ANY),
            pl.BlockSpec(memory_space=pl.ANY),
        ),
        scratch_shapes=[
            *[vmem(blocks, BF16) for _ in range(8)],
            vmem((8, SIDE, 2, TILE, HALF), BF16),
            vmem(pairs, BF16),
            vmem(pairs, BF16),
            vmem((ROWS, HALF), BF16),
            vmem((ROWS, HALF), BF16),
            vmem((HALF, ROWS), BF16),
            vmem((HALF, ROWS), BF16),
            vmem((SIDE, SIDE, PAIR, ROWS), BF16),
            vmem((2, HALF, HALF), F32),
            vmem((4, 4, TILE, HALF), BF16),
            vmem((4, 4, TILE, HALF), BF16),
            vmem((4, 4, TILE, HALF), BF16),
            vmem((4, 4, TILE, HALF), BF16),
            vmem((BLOCKS, 16, HALF), F32),
            vmem((PAIR, HALF), F32),
            vmem((4, 2, COLS, HALF), BF16),
            vmem((1, ROWS), I32),
            *[vmem((1, ROWS), F32) for _ in range(4)],
            vmem((8, TILE), I32),
            vmem((8, 8, TILE), I32),
            vmem((4, 8, TILE), I32),
            pltpu.SMEM((8, TILE), I32),
            pltpu.SMEM((8, 8, TILE), I32),
            pltpu.SMEM((4, 8, TILE), I32),
            dma(4),
            dma(2),
            dma(4, 2),
            dma(4),
            pltpu.SemaphoreType.DMA,
            dma(8),
            dma(8),
            dma(2, 4),
            dma(2, 4),
            dma(4),
            dma(4),
            dma(8, 4),
            dma(4, 4),
            dma(4, 4),
            dma(8, 4),
            dma(4, 4, 2),
            dma(4),
            dma(4),
            dma(2, 4),
            dma(2, 4),
            dma(4),
            dma(4),
            pltpu.SemaphoreType.DMA,
            pltpu.SemaphoreType.DMA,
        ],
        compiler_params=pltpu.CompilerParams(
            collective_id=0, has_side_effects=True, vmem_limit_bytes=62 * 2**20
        ),
    )(designs, prototypes, candidates, positives.reshape(1, ROWS))
    return losses.reshape(ROWS), design_grad, proto_grad


def solution(mesh):
    return jax.shard_map(
        body,
        mesh=mesh,
        in_specs=(
            P(("proto", "design"), None),
            P("proto", None),
            P(("proto", "design"), None),
            P(("proto", "design")),
        ),
        out_specs=(
            P(("proto", "design")),
            P(("proto", "design"), None),
            P(("proto", "design"), None),
        ),
        check_vma=False,
    )
```

time: 521 us -> 217 us (0.42)
  Pallas kernels: 0 us -> 211 us
  blocking collectives: 189 us -> 0 us
  waiting for transfers between devices: 179 us -> 0 us
  local copies, waits for them, and re-layouts: 50.7 us -> 5.42 us
  matrix products: 38.1 us -> 0 us
  other arithmetic: 32 us -> 0 us
  starting transfers between devices: 14.1 us -> 0 us
  between operations: 14.2 us -> 0.64 us
    pallas_call x0 -> x1, Pallas kernels: none -> 211 us  [body(): pl.pallas_call(kernel, out_shape=(jax.ShapeDtypeStruct((1, ROWS), F32), j...]
    all_to_all x1 -> x0, blocking collectives: 189 us -> none  [body(): lax.all_to_all(outgoing_grad, 'proto', split_axis=0, concat_axis=0, tiled...]
    all_to_all x2 -> x0, waiting for transfers between devices: 138 us -> none  [the longest x1 137 us: body(): lax.all_to_all(outgoing, 'proto', split_axis=0, concat_axis=0, tiled=True)]
    reduce_scatter x1 -> x0, waiting for transfers between devices: 41.6 us -> none  [body(): lax.psum_scatter(summed, 'design', scatter_dimension=0, tiled=True)]
    dot_general x4 -> x0, matrix products: 38.1 us -> none  [the longest x1 13.7 us: contrast(): jnp.dot(logit_grad, cand_rows, preferred_element_type=jnp.float32)]
    gather x3 -> x0, local copies, waits for them, and re-layouts: 27.9 us -> none  [the longest x1 12.9 us: body(): jnp.take(tile_grad, source, axis=0)]
    select_n x7 -> x0, other arithmetic: 19.5 us -> none  [the longest x1 7.57 us: body(): jnp.where((incoming >= 0)[:, None, None], fetched, jnp.zeros((), jnp.bflo...]
    all_to_all x2 -> x0, starting transfers between devices: 13.9 us -> none  [the longest x1 7.6 us: body(): lax.all_to_all(requested, 'proto', split_axis=0, concat_axis=0, tiled=True)]
  transfers between devices with their start and end apart: 3 -> 0, of which waited for: 3 -> 0; matrix products, arithmetic and copies ran while one was open for 4% -> 0% of each run, Pallas kernels for 0% -> 0%
where the time goes in v1:
time: 217 us
  Pallas kernels  211 us (97%)
  local copies, waits for them, and re-layouts  5.42 us (2%)
    pallas_call x1, Pallas kernels, body(): pl.pallas_call(kernel, out_shape=(jax.ShapeDtypeStruct((1, ROWS), F32), j...  211 us
    unnamed x5, local copies, waits for them, and re-layouts  5.42 us

profile of v1, /device:TPU:9, one launch (start us, length us, event | category | flops | bytes accessed | tf_op | source)
XLA Modules:
  0.0 216.6 jit_solution(15222963997435566934)
XLA Ops:
  0.6 210.5 %shard_map.67 = (f32[1,1024]{1,0:T(1,128)}, bf16[1024,1024]{1,0:T(8,128)(2,1)}, f32[256,1024]{1,0:T(8,128)}) custom-call(bf16[1024,1024]{1,0:T(8,128)(2,1)} %des.1, f32[2048,1024]{1,0:T(8,128)} %proto.1, s32[1,24]{1,0:T(1,128)} %cand.1, s32[1,1024]{1,0:T(1,128)} %bitcast.2), custom_call_target="tpu_custom_call" | custom-call | tf_op jit(solution)/shard_map/pallas_call | solution.py:440
  211.2 1.3 copy.10
  212.5 0.0 copy-start
  212.5 3.2 %copy.11 = bf16[1024,1024]{1,0:T(8,128)(2,1)} copy(bf16[1024,1024]{1,0:T(8,128)(2,1)} %get-tuple-element.13) | data formatting | bytes 4194304
  215.6 0.0 copy-done
  215.6 1.0 copy.12
Async XLA Ops:
  212.5 3.2 %copy-start = (f32[256,1024]{1,0:T(8,128)S(1)}, f32[256,1024]{1,0:T(8,128)}, u32[]{:S(2)}) copy-start(f32[256,1024]{1,0:T(8,128)} %get-tuple-element.14) | copy-start | bytes 3145732

commit v2 on v1

--- a/solution.py
+++ b/solution.py
@@ -48,16 +48,17 @@
 def pair_of(n):
     s = jnp.where(n >= 1, 1, 0) + jnp.where(n >= 4, 1, 0) + jnp.where(n >= 9, 1, 0)
     m = n - s * s
-    return gray(jnp.minimum(s, 2 * s - m)), gray(jnp.minimum(m, s))
+    odd = m % 2
+    return gray(s + odd * (m // 2 - s)), gray(m // 2 + odd * (s - m // 2))
 
 
 def kernel(
     des, proto, cand, pos, loss_o, dg_o, pg_o,
     tab0, tab1, tab2, tab3, rr0, rr1, rr2, rr3,
-    send, arr_m, arr_o, des_m, des_o, dt_m, dt_o, grads, stage, merge, from_up, from_down, from_y, runs, core_in, dg_s,
+    send, arr_m, arr_o, des_m, des_o, dt_m, dt_o, grads, stage, merge, from_up, from_down, from_y, far_y, runs, core_in, dg_s,
     prow, m_run, s_run, pick, total, req_v, req_in, order_v, req_own, req_s, order_s,
-    ld_sem, des_sem, out_sem, loc_sem, own_sem, rq_s, rq_r, ag_s, ag_r, rl_s, rl_r, f_s, fm_r, fo_r, b_s, b_r,
-    mg_s, mg_r, rs_s, rs_r, y_s, y_r, c_s, c_r,
+    ld_sem, des_sem, out_sem, loc_sem, own_sem, rq_s, rq_r, ag_s, ag_r, rl_s, rl_r, gy_s, gy_r, f_s, fm_r, fo_r, b_s, b_r,
+    fy_s, fy_r, mg_s, mg_r, rs_s, rs_r, y_s, y_r, c_s, c_r,
 ):
     p, d = lax.axis_index("proto"), lax.axis_index("design")
     x, z, y, r = p // SIDE, p % SIDE, d // 2, d % 2
@@ -72,12 +73,19 @@
     def along_v(k, core):
         return (owner(0, k), y * 2 + core)
 
+    def along_y(k):
+        return (p, ((y + k) % SIDE) * 2 + r)
+
+    def group(k):
+        return pl.ds(((y + k) % SIDE) * 4, 4)
+
     sibling = (p, y * 2 + 1 - r)
     my_cols = pl.ds(pl.multiple_of(r * HALF, HALF), HALF)
     other_cols = pl.ds(pl.multiple_of((1 - r) * HALF, HALF), HALF)
 
     def load(k):
-        return pltpu.make_async_copy(proto.at[pl.ds(k * HALF, HALF), my_cols], stage.at[k % 2], ld_sem.at[k])
+        rows = pl.ds(pl.multiple_of(((y + k) % SIDE) * HALF, HALF), HALF)
+        return pltpu.make_async_copy(proto.at[rows, my_cols], stage.at[k % 2], ld_sem.at[k])
 
     load(0).start()
     load(1).start()
@@ -91,7 +99,7 @@
     barrier = pltpu.get_barrier_semaphore()
     partners = [sibling]
     for k in (1, 2, 3):
-        partners += [along_v(k, r), along_v(k, 1 - r), along_u(k, 1 - r), (p, ((y + k) % SIDE) * 2 + r)]
+        partners += [along_v(k, r), along_v(k, 1 - r), along_u(k, 1 - r), along_y(k)]
     partners += [along_u(1, r), along_u(3, r)]
     for q in partners:
         pl.semaphore_signal(barrier, inc=1, device_id=q, device_id_type=MESH)
@@ -121,17 +129,17 @@
         c.start()
 
     def own_chunk(k, way):
-        part = pl.ds(4 * k, 4)
+        part = group(k)
         dst = tab3 if way == 0 else tab1
         return remote(tab0.at[part], dst.at[part], ag_s.at[way, k], ag_r.at[way, k], along_u(1 if way == 0 else 3, r))
 
     for k in range(4):
         load(k).wait()
         for b in range(4):
-            tab0[4 * k + b] = stage[k % 2, TILE * b : TILE * (b + 1)].astype(BF16)
-        own_chunk(k, 0).start()
-        own_chunk(k, 1).start()
+            tab0[((y + k) % SIDE) * 4 + b] = stage[k % 2, TILE * b : TILE * (b + 1)].astype(BF16)
         if k < 2:
+            own_chunk(k, 0).start()
+            own_chunk(k, 1).start()
             load(k + 2).start()
 
     for c in designs_in:
@@ -151,8 +159,7 @@
 
     def wanted_blocks(ku):
         first = owner(ku, 0) * 2
-        for n in range(8):
-            k, so = n // 2, n % 2
+        for n in (0, 2, 3, 6, 7, 1, 4, 5):
             for i in range(2):
                 val = tab[ku][jnp.maximum(req_s[n, 0, first + i], 0)]
                 if n == 0:
@@ -169,28 +176,33 @@
             return remote(send.at[n, ku], arr_m.at[back, ku], f_s.at[n, ku], fm_r.at[back, ku], along_v(k, r))
         return remote(send.at[n, ku], arr_o.at[back, ku], f_s.at[n, ku], fo_r.at[back, ku], along_v(k, 1 - r))
 
-    def relay(k):
-        part = pl.ds(4 * k, 4)
-        src, to = (tab3, 1) if k < 2 else (tab1, 3)
-        return remote(src.at[part], tab2.at[part], rl_s.at[k], rl_r.at[k], along_u(to, r))
-
-    def pass_on(k):
-        own_chunk(k, 0 if k < 2 else 1).wait_recv()
-        relay(k).start()
-
-    pass_on(0)
+    def relay(way):
+        part = pl.ds(4 * y + 2 * way, 2)
+        src, to = (tab3, 1) if way == 0 else (tab1, 3)
+        return remote(src.at[part], tab2.at[part], rl_s.at[way], rl_r.at[way], along_u(to, r))
+
+    def share(k):
+        return remote(tab2.at[group(0)], tab2.at[group(0)], gy_s.at[k], gy_r.at[SIDE - k], along_y(k))
+
+    for way in (0, 1):
+        own_chunk(0, way).wait_recv()
+        relay(way).start()
+    for k in (2, 3):
+        own_chunk(k, 0).start()
+        own_chunk(k, 1).start()
+    for way in (0, 1):
+        relay(way).wait_recv()
+    for k in (1, 3, 2):
+        share(k).start()
     wanted_blocks(0)
-    pass_on(1)
-    own_chunk(0, 1).wait_recv()
-    own_chunk(1, 1).wait_recv()
-    pass_on(2)
-    own_chunk(2, 0).wait_recv()
-    pass_on(3)
-    own_chunk(3, 0).wait_recv()
+    for k in (1, 2, 3):
+        own_chunk(k, 1).wait_recv()
     wanted_blocks(1)
+    for k in (1, 2, 3):
+        own_chunk(k, 0).wait_recv()
     wanted_blocks(3)
-    for k in range(4):
-        relay(k).wait_recv()
+    for k in (1, 2, 3):
+        remote(tab2.at[group(0)], tab2.at[group(0)], gy_s.at[k], gy_r.at[k], sibling).wait_recv()
     wanted_blocks(2)
 
     for ku in range(4):
@@ -262,7 +274,10 @@
     for k in range(4):
         own_chunk(k, 0).wait_send()
         own_chunk(k, 1).wait_send()
-        relay(k).wait_send()
+    for way in (0, 1):
+        relay(way).wait_send()
+    for k in (1, 2, 3):
+        share(k).wait_send()
 
     def back_mine(ku, kv, k):
         back = (SIDE - kv) % SIDE
@@ -321,75 +336,91 @@
                 val = runs[order_s[ku, 2, j]]
                 tab[ku][j, part, :] = jnp.where(order_s[ku, 3, j] > 0, val, 0.0).astype(BF16)
 
-    def design_grad(q):
+    def design_grad(q, h):
         part = pl.ds(q * COLS, COLS)
-        for h in range(2):
-            acc = stage.at[0, pl.ds(0, COLS)]
-            acc[...] = jnp.zeros((COLS, HALF), F32)
-
-            @pl.loop(0, 4)
-            def _(k):
-                lhs = grads[k, :, :, part] if h == 0 else grads[:, k, :, part]
-                rhs = arr_m[k] if h == 0 else arr_o[k]
-                acc[...] += lax.dot_general(
-                    lhs.reshape(ROWS, COLS), rhs.reshape(ROWS, HALF), (((0,), (0,)), ((), ())), preferred_element_type=F32
-                )
-
-            dg_s[q, h] = acc[...].astype(BF16)
-            dg_out(q, h).start()
+        acc = stage.at[0, pl.ds(0, COLS)]
+        acc[...] = jnp.zeros((COLS, HALF), F32)
+
+        @pl.loop(0, 4)
+        def _(k):
+            lhs = grads[k, :, :, part] if h == 0 else grads[:, k, :, part]
+            rhs = arr_m[k] if h == 0 else arr_o[k]
+            acc[...] += lax.dot_general(
+                lhs.reshape(ROWS, COLS), rhs.reshape(ROWS, HALF), (((0,), (0,)), ((), ())), preferred_element_type=F32
+            )
+
+        dg_s[q, h] = acc[...].astype(BF16)
+        dg_out(q, h).start()
 
     def dg_out(q, h):
         cols = my_cols if h == 0 else other_cols
         return pltpu.make_async_copy(dg_s.at[q, h], dg_o.at[pl.ds(q * COLS, COLS), cols], out_sem.at[q, h])
 
-    def far(g):
-        part = pl.ds(4 * g, 4)
-        return remote(tab2.at[part], merge.at[g], mg_s.at[g], mg_r.at[g], along_u(1 if g < 2 else 3, r))
-
-    def near(g, way):
-        part = pl.ds(4 * g, 4)
+    def far_along_y(k):
+        return remote(tab2.at[group(k)], far_y.at[SIDE - k], fy_s.at[k], fy_r.at[SIDE - k], along_y(k))
+
+    def far(way):
+        part = pl.ds(4 * y + 2 * way, 2)
+        return remote(tab2.at[part], merge.at[way], mg_s.at[way], mg_r.at[way], along_u(1 if way == 0 else 3, r))
+
+    def near(k, way):
         if way == 0:
-            return remote(tab1.at[part], from_down.at[g], rs_s.at[0, g], rs_r.at[0, g], along_u(1, r))
-        return remote(tab3.at[part], from_up.at[g], rs_s.at[1, g], rs_r.at[1, g], along_u(3, r))
-
-    def merged(g):
-        src = tab1 if g < 2 else tab3
-        far(g).wait_recv()
+            return remote(tab1.at[group(k)], from_down.at[k], rs_s.at[0, k], rs_r.at[0, k], along_u(1, r))
+        return remote(tab3.at[group(k)], from_up.at[k], rs_s.at[1, k], rs_r.at[1, k], along_u(3, r))
+
+    def to_y(k):
+        return remote(tab0.at[group(k)], from_y.at[SIDE - k], y_s.at[k], y_r.at[SIDE - k], along_y(k))
+
+    sums(2)
+    for k in (1, 3, 2):
+        far_along_y(k).start()
+    design_grad(0, 0)
+    design_grad(0, 1)
+    design_grad(1, 0)
+    sums(3)
+    for k in (1, 3, 2):
+        near(k, 1).start()
+    sums(1)
+    for k in (1, 3, 2):
+        near(k, 0).start()
+    sums(0)
+    design_grad(1, 1)
+    design_grad(2, 0)
+    for k in (1, 3, 2):
+        remote(tab2.at[group(0)], far_y.at[k], fy_s.at[k], fy_r.at[k], sibling).wait_recv()
+    for b in range(4):
+        val = tab2[4 * y + b].astype(F32)
+        for k in (1, 2, 3):
+            val += far_y[k, b].astype(F32)
+        tab2[4 * y + b] = val.astype(BF16)
+    far(0).start()
+    far(1).start()
+
+    def add_near(k):
+        near(k, 0).wait_recv()
+        near(k, 1).wait_recv()
         for b in range(4):
-            src[4 * g + b] = (src[4 * g + b].astype(F32) + merge[g, b].astype(F32)).astype(BF16)
-        near(g, 0 if g < 2 else 1).start()
-
-    sums(2)
-    for g in (0, 2, 1, 3):
-        far(g).start()
-    design_grad(0)
-    sums(1)
-    near(2, 0).start()
-    near(3, 0).start()
-    sums(3)
-    near(0, 1).start()
-    near(1, 1).start()
-    for g in (0, 2, 1, 3):
-        merged(g)
-    sums(0)
-    design_grad(1)
-    design_grad(2)
-
-    def to_y(g):
-        return remote(tab0.at[pl.ds(4 * g, 4)], from_y.at[(y - g + SIDE) % SIDE], y_s.at[g], y_r.at[(y - g + SIDE) % SIDE], (p, g * 2 + r))
-
-    for g in (0, 2, 1, 3):
-        near(g, 0).wait_recv()
-        near(g, 1).wait_recv()
-        for b in range(4):
-            val = tab0[4 * g + b].astype(F32) + from_up[g, b].astype(F32) + from_down[g, b].astype(F32)
-            tab0[4 * g + b] = val.astype(BF16)
-
-        @pl.when(y != g)
-        def _():
-            to_y(g).start()
-
-    design_grad(3)
+            at = ((y + k) % SIDE) * 4 + b
+            val = tab0[at].astype(F32) + from_up[k, b].astype(F32) + from_down[k, b].astype(F32)
+            tab0[at] = val.astype(BF16)
+
+    add_near(1)
+    to_y(1).start()
+    for way in (0, 1):
+        src = tab1 if way == 0 else tab3
+        far(way).wait_recv()
+        for b in range(2):
+            at = 4 * y + 2 * way + b
+            src[at] = (src[at].astype(F32) + merge[way, b].astype(F32)).astype(BF16)
+        near(0, way).start()
+    design_grad(2, 1)
+    add_near(3)
+    to_y(3).start()
+    design_grad(3, 0)
+    add_near(2)
+    to_y(2).start()
+    design_grad(3, 1)
+    add_near(0)
     for k in (1, 3, 2):
         remote(tab0.at[pl.ds(0, 4)], from_y.at[k], y_s.at[0], y_r.at[k], sibling).wait_recv()
 
@@ -416,19 +447,37 @@
             if kv:
                 back_mine(ku, kv, ku).wait_send()
             back_other(ku, kv, kv).wait_send()
-    for g in range(4):
-        far(g).wait_send()
-        near(g, 0).wait_send()
-        near(g, 1).wait_send()
-
-        @pl.when(y != g)
-        def _():
-            to_y(g).wait_send()
-
+    for k in range(4):
+        near(k, 0).wait_send()
+        near(k, 1).wait_send()
+        if k:
+            far_along_y(k).wait_send()
+            to_y(k).wait_send()
         for h in range(2):
-            dg_out(g, h).wait()
+            dg_out(k, h).wait()
+    far(0).wait_send()
+    far(1).wait_send()
     cross.wait_send()
     for c in outs:
+        c.wait()
+
+
+def settle(losses, design_grad, proto_grad, losses_o, design_grad_o, proto_grad_o, one, many, few, sems):
+    moves = [(losses, one, losses_o)]
+    for i in range(4):
+        part = pl.ds(i * COLS, COLS)
+        moves.append((design_grad.at[part], many.at[part], design_grad_o.at[part]))
+    for i in range(2):
+        part = pl.ds(i * TILE, TILE)
+        moves.append((proto_grad.at[part], few.at[part], proto_grad_o.at[part]))
+    reads = [pltpu.make_async_copy(a, b, sems.at[0, n]) for n, (a, b, c) in enumerate(moves)]
+    writes = [pltpu.make_async_copy(b, c, sems.at[1, n]) for n, (a, b, c) in enumerate(moves)]
+    for c in reads:
+        c.start()
+    for a, b in zip(reads, writes):
+        a.wait()
+        b.start()
+    for c in writes:
         c.wait()
 
 
@@ -466,6 +515,7 @@
             vmem((HALF, ROWS), BF16),
             vmem((SIDE, SIDE, PAIR, ROWS), BF16),
             vmem((2, HALF, HALF), F32),
+            vmem((2, 2, TILE, HALF), BF16),
             vmem((4, 4, TILE, HALF), BF16),
             vmem((4, 4, TILE, HALF), BF16),
             vmem((4, 4, TILE, HALF), BF16),
@@ -490,6 +540,8 @@
             dma(8),
             dma(2, 4),
             dma(2, 4),
+            dma(2),
+            dma(2),
             dma(4),
             dma(4),
             dma(8, 4),
@@ -499,6 +551,8 @@
             dma(4, 4, 2),
             dma(4),
             dma(4),
+            dma(2),
+            dma(2),
             dma(2, 4),
             dma(2, 4),
             dma(4),
@@ -510,6 +564,17 @@
             collective_id=0, has_side_effects=True, vmem_limit_bytes=62 * 2**20
         ),
     )(designs, prototypes, candidates, positives.reshape(1, ROWS))
+    losses, design_grad, proto_grad = pl.pallas_call(
+        settle,
+        out_shape=(
+            jax.ShapeDtypeStruct((1, ROWS), F32),
+            jax.ShapeDtypeStruct((ROWS, D), BF16),
+            jax.ShapeDtypeStruct((PAIR, D), F32),
+        ),
+        in_specs=[pl.BlockSpec(memory_space=pl.ANY)] * 3,
+        out_specs=(pl.BlockSpec(memory_space=pl.ANY),) * 3,
+        scratch_shapes=[vmem((1, ROWS), F32), vmem((ROWS, D), BF16), vmem((PAIR, D), F32), dma(2, 7)],
+    )(losses, design_grad, proto_grad)
     return losses.reshape(ROWS), design_grad, proto_grad
 
 

time: 217 us -> 188 us (0.87)
  Pallas kernels: 211 us -> 187 us
  local copies, waits for them, and re-layouts: 5.42 us -> 0 us
    pallas_call x1, Pallas kernels: 211 us -> 184 us  [body(): pl.pallas_call(kernel, out_shape=(jax.ShapeDtypeStruct((1, ROWS), F32), j...]
    unnamed x5 -> x0, local copies, waits for them, and re-layouts: 5.42 us -> none
    pallas_call x0 -> x1, Pallas kernels: none -> 2.82 us  [body(): pl.pallas_call(settle, out_shape=(jax.ShapeDtypeStruct((1, ROWS), F32), j...]
where the time goes in v2:
time: 188 us; the launch traced here: 187 us
  Pallas kernels  187 us (99%)
    pallas_call x1, Pallas kernels, body(): pl.pallas_call(kernel, out_shape=(jax.ShapeDtypeStruct((1, ROWS), F32), j...  184 us

profile of v2, /device:TPU:9, one launch (start us, length us, event | category | flops | bytes accessed | tf_op | source)
XLA Modules:
  0.0 187.4 jit_solution(13325474558912674114)
XLA Ops:
  0.6 183.9 %shard_map.67 = (f32[1,1024]{1,0:T(1,128)}, bf16[1024,1024]{1,0:T(8,128)(2,1)}, f32[256,1024]{1,0:T(8,128)}) custom-call(bf16[1024,1024]{1,0:T(8,128)(2,1)} %des.1, f32[2048,1024]{1,0:T(8,128)} %proto.1, s32[1,24]{1,0:T(1,128)} %cand.1, s32[1,1024]{1,0:T(1,128)} %bitcast.2), custom_call_target="tpu_custom_call" | custom-call | tf_op jit(solution)/shard_map/pallas_call | solution.py:489
  184.6 2.8 %shard_map.68 = (f32[1,1024]{1,0:T(1,128)}, bf16[1024,1024]{1,0:T(8,128)(2,1)}, f32[256,1024]{1,0:T(8,128)}) custom-call(f32[1,1024]{1,0:T(1,128)} %get-tuple-element.9.losses, bf16[1024,1024]{1,0:T(8,128)(2,1)} %get-tuple-element.10.design_grad, f32[256,1024]{1,0:T(8,128)} %get-tuple-element.11.proto_grad), custom_call_target="tpu_custom_call" | custom-call | tf_op jit(solution)/shard_map/pallas_call | solution.py:567

commit v3 on v2

--- a/solution.py
+++ b/solution.py
@@ -57,7 +57,7 @@
     tab0, tab1, tab2, tab3, rr0, rr1, rr2, rr3,
     send, arr_m, arr_o, des_m, des_o, dt_m, dt_o, grads, stage, merge, from_up, from_down, from_y, far_y, runs, core_in, dg_s,
     prow, m_run, s_run, pick, total, req_v, req_in, order_v, req_own, req_s, order_s,
-    ld_sem, des_sem, out_sem, loc_sem, own_sem, rq_s, rq_r, ag_s, ag_r, rl_s, rl_r, gy_s, gy_r, f_s, fm_r, fo_r, b_s, b_r,
+    ld_sem, des_sem, out_sem, loc_sem, own_sem, rq_s, rq_r, ag_s, ag_r, rl_s, rl_r, gy_s, gy_r, ha_s, ha_r, f_s, fm_r, fo_r, b_s, b_r,
     fy_s, fy_r, mg_s, mg_r, rs_s, rs_r, y_s, y_r, c_s, c_r,
 ):
     p, d = lax.axis_index("proto"), lax.axis_index("design")
@@ -83,9 +83,11 @@
     my_cols = pl.ds(pl.multiple_of(r * HALF, HALF), HALF)
     other_cols = pl.ds(pl.multiple_of((1 - r) * HALF, HALF), HALF)
 
-    def load(k):
-        rows = pl.ds(pl.multiple_of(((y + k) % SIDE) * HALF, HALF), HALF)
-        return pltpu.make_async_copy(proto.at[rows, my_cols], stage.at[k % 2], ld_sem.at[k])
+    turns = (0, 1, 3, 2)
+
+    def load(j):
+        rows = pl.ds(pl.multiple_of(((y + turns[j]) % SIDE) * HALF, HALF), HALF)
+        return pltpu.make_async_copy(proto.at[rows, my_cols], stage.at[j % 2], ld_sem.at[j])
 
     load(0).start()
     load(1).start()
@@ -129,18 +131,19 @@
         c.start()
 
     def own_chunk(k, way):
-        part = group(k)
+        low, count = ((0, 4), (2, 2), (0, 4), (0, 2))[k]
+        part = pl.ds(((y + k) % SIDE) * 4 + low, count)
         dst = tab3 if way == 0 else tab1
         return remote(tab0.at[part], dst.at[part], ag_s.at[way, k], ag_r.at[way, k], along_u(1 if way == 0 else 3, r))
 
-    for k in range(4):
-        load(k).wait()
+    for j in range(4):
+        load(j).wait()
         for b in range(4):
-            tab0[((y + k) % SIDE) * 4 + b] = stage[k % 2, TILE * b : TILE * (b + 1)].astype(BF16)
-        if k < 2:
-            own_chunk(k, 0).start()
-            own_chunk(k, 1).start()
-            load(k + 2).start()
+            tab0[((y + turns[j]) % SIDE) * 4 + b] = stage[j % 2, TILE * b : TILE * (b + 1)].astype(BF16)
+        if j < 2:
+            own_chunk(turns[j], 0).start()
+            own_chunk(turns[j], 1).start()
+            load(j + 2).start()
 
     for c in designs_in:
         c.wait()
@@ -184,10 +187,17 @@
     def share(k):
         return remote(tab2.at[group(0)], tab2.at[group(0)], gy_s.at[k], gy_r.at[SIDE - k], along_y(k))
 
+    def hand(way, k):
+        part = pl.ds(4 * y + (2 if k == 1 else 0), 2)
+        src = tab3 if way == 0 else tab1
+        return remote(src.at[part], src.at[part], ha_s.at[way, k // 2], ha_r.at[way, k // 2], along_y(k))
+
     for way in (0, 1):
         own_chunk(0, way).wait_recv()
         relay(way).start()
-    for k in (2, 3):
+        hand(way, 1).start()
+        hand(way, 3).start()
+    for k in (3, 2):
         own_chunk(k, 0).start()
         own_chunk(k, 1).start()
     for way in (0, 1):
@@ -195,12 +205,12 @@
     for k in (1, 3, 2):
         share(k).start()
     wanted_blocks(0)
-    for k in (1, 2, 3):
-        own_chunk(k, 1).wait_recv()
-    wanted_blocks(1)
-    for k in (1, 2, 3):
-        own_chunk(k, 0).wait_recv()
-    wanted_blocks(3)
+    for way, ku in ((1, 1), (0, 3)):
+        for k in (1, 2, 3):
+            own_chunk(k, way).wait_recv()
+        hand(way, 1).wait_recv()
+        hand(way, 3).wait_recv()
+        wanted_blocks(ku)
     for k in (1, 2, 3):
         remote(tab2.at[group(0)], tab2.at[group(0)], gy_s.at[k], gy_r.at[k], sibling).wait_recv()
     wanted_blocks(2)
@@ -276,6 +286,8 @@
         own_chunk(k, 1).wait_send()
     for way in (0, 1):
         relay(way).wait_send()
+        hand(way, 1).wait_send()
+        hand(way, 3).wait_send()
     for k in (1, 2, 3):
         share(k).wait_send()
 
@@ -287,8 +299,7 @@
         back = (SIDE - ku) % SIDE
         return remote(send.at[ku * 2 + 1, kv], rr[k].at[pl.ds(back * 4 + 2, 2)], b_s.at[ku * 2 + 1, kv], b_r.at[k, back, 1], along_u(ku, 1 - r))
 
-    @pl.loop(0, 16)
-    def _(n):
+    def second_pass(n):
         ku, kv = pair_of(15 - n)
 
         @pl.loop(0, ROWS // COLS)
@@ -316,8 +327,6 @@
             @pl.when(kv == k)
             def _():
                 back_other(ku, kv, k).start()
-
-    order_copy.wait()
 
     def sums(ku):
         for n in range(1, 8):
@@ -371,21 +380,22 @@
     def to_y(k):
         return remote(tab0.at[group(k)], from_y.at[SIDE - k], y_s.at[k], y_r.at[SIDE - k], along_y(k))
 
+    pl.loop(0, 12)(second_pass)
+    order_copy.wait()
     sums(2)
     for k in (1, 3, 2):
         far_along_y(k).start()
+    pl.loop(12, 16)(second_pass)
     design_grad(0, 0)
     design_grad(0, 1)
+    sums(3)
+    near(1, 1).start()
+    near(3, 1).start()
     design_grad(1, 0)
-    sums(3)
-    for k in (1, 3, 2):
-        near(k, 1).start()
     sums(1)
-    for k in (1, 3, 2):
-        near(k, 0).start()
+    near(1, 0).start()
+    near(3, 0).start()
     sums(0)
-    design_grad(1, 1)
-    design_grad(2, 0)
     for k in (1, 3, 2):
         remote(tab2.at[group(0)], far_y.at[k], fy_s.at[k], fy_r.at[k], sibling).wait_recv()
     for b in range(4):
@@ -395,6 +405,9 @@
         tab2[4 * y + b] = val.astype(BF16)
     far(0).start()
     far(1).start()
+    near(2, 0).start()
+    near(2, 1).start()
+    design_grad(1, 1)
 
     def add_near(k):
         near(k, 0).wait_recv()
@@ -406,6 +419,8 @@
 
     add_near(1)
     to_y(1).start()
+    add_near(3)
+    to_y(3).start()
     for way in (0, 1):
         src = tab1 if way == 0 else tab3
         far(way).wait_recv()
@@ -413,12 +428,11 @@
             at = 4 * y + 2 * way + b
             src[at] = (src[at].astype(F32) + merge[way, b].astype(F32)).astype(BF16)
         near(0, way).start()
-    design_grad(2, 1)
-    add_near(3)
-    to_y(3).start()
-    design_grad(3, 0)
+    design_grad(2, 0)
     add_near(2)
     to_y(2).start()
+    design_grad(2, 1)
+    design_grad(3, 0)
     design_grad(3, 1)
     add_near(0)
     for k in (1, 3, 2):
@@ -544,6 +558,8 @@
             dma(2),
             dma(4),
             dma(4),
+            dma(2, 2),
+            dma(2, 2),
             dma(8, 4),
             dma(4, 4),
             dma(4, 4),

time: 188 us -> 174 us (0.926)
  Pallas kernels: 187 us -> 173 us
    pallas_call x1, Pallas kernels: 184 us -> 170 us  [body(): pl.pallas_call(kernel, out_shape=(jax.ShapeDtypeStruct((1, ROWS), F32), j...]
where the time goes in v3:
time: 174 us
  Pallas kernels  173 us (99%)
    pallas_call x1, Pallas kernels, body(): pl.pallas_call(kernel, out_shape=(jax.ShapeDtypeStruct((1, ROWS), F32), j...  170 us

profile of v3, /device:TPU:9, one launch (start us, length us, event | category | flops | bytes accessed | tf_op | source)
XLA Modules:
  0.0 173.7 jit_solution(7343935211515463656)
XLA Ops:
  0.6 170.2 %shard_map.67 = (f32[1,1024]{1,0:T(1,128)}, bf16[1024,1024]{1,0:T(8,128)(2,1)}, f32[256,1024]{1,0:T(8,128)}) custom-call(bf16[1024,1024]{1,0:T(8,128)(2,1)} %des.1, f32[2048,1024]{1,0:T(8,128)} %proto.1, s32[1,24]{1,0:T(1,128)} %cand.1, s32[1,1024]{1,0:T(1,128)} %bitcast.2), custom_call_target="tpu_custom_call" | custom-call | tf_op jit(solution)/shard_map/pallas_call | solution.py:503
  170.9 2.8 %shard_map.68 = (f32[1,1024]{1,0:T(1,128)}, bf16[1024,1024]{1,0:T(8,128)(2,1)}, f32[256,1024]{1,0:T(8,128)}) custom-call(f32[1,1024]{1,0:T(1,128)} %get-tuple-element.9.losses, bf16[1024,1024]{1,0:T(8,128)(2,1)} %get-tuple-element.10.design_grad, f32[256,1024]{1,0:T(8,128)} %get-tuple-element.11.proto_grad), custom_call_target="tpu_custom_call" | custom-call | tf_op jit(solution)/shard_map/pallas_call | solution.py:583

commit v4 on v3

--- a/solution.py
+++ b/solution.py
@@ -312,17 +312,20 @@
         send[kv * 2, ku] = mine
         other = jnp.dot(grads[kv, ku], des_o[...], preferred_element_type=F32).astype(BF16).reshape(2, TILE, HALF)
         send[ku * 2 + 1, kv] = other
-        for k in range(4):
-
-            @pl.when(ku == k)
+
+        @pl.when((ku == 0) & (kv == 0))
+        def _():
+            rr[0][0:2] = send[0, 0]
+
+        for k in (1, 2, 3):
+
+            @pl.when((ku == k) & (kv == 0))
             def _():
-                @pl.when(kv == 0)
-                def _():
-                    rr[k][0:2] = send[0, k]
-
-                @pl.when(kv != 0)
-                def _():
-                    back_mine(ku, kv, k).start()
+                rr[k][0:2] = send[0, k]
+
+            @pl.when((ku == k) & (kv != 0))
+            def _():
+                back_mine(ku, kv, k).start()
 
             @pl.when(kv == k)
             def _():
@@ -386,16 +389,20 @@
     for k in (1, 3, 2):
         far_along_y(k).start()
     pl.loop(12, 16)(second_pass)
+    for kv in (1, 3, 2):
+        back_mine(0, kv, 0).start()
     design_grad(0, 0)
+    sums(3)
+    near(2, 1).start()
+    sums(1)
+    near(2, 0).start()
+    for ku in (0, 1, 3, 2):
+        back_other(ku, 0, 0).start()
+    for k in (1, 3):
+        near(k, 1).start()
+        near(k, 0).start()
     design_grad(0, 1)
-    sums(3)
-    near(1, 1).start()
-    near(3, 1).start()
     design_grad(1, 0)
-    sums(1)
-    near(1, 0).start()
-    near(3, 0).start()
-    sums(0)
     for k in (1, 3, 2):
         remote(tab2.at[group(0)], far_y.at[k], fy_s.at[k], fy_r.at[k], sibling).wait_recv()
     for b in range(4):
@@ -405,9 +412,8 @@
         tab2[4 * y + b] = val.astype(BF16)
     far(0).start()
     far(1).start()
-    near(2, 0).start()
-    near(2, 1).start()
     design_grad(1, 1)
+    sums(0)
 
     def add_near(k):
         near(k, 0).wait_recv()
@@ -417,8 +423,12 @@
             val = tab0[at].astype(F32) + from_up[k, b].astype(F32) + from_down[k, b].astype(F32)
             tab0[at] = val.astype(BF16)
 
+    add_near(2)
+    to_y(2).start()
+    design_grad(2, 0)
     add_near(1)
     to_y(1).start()
+    design_grad(2, 1)
     add_near(3)
     to_y(3).start()
     for way in (0, 1):
@@ -428,10 +438,6 @@
             at = 4 * y + 2 * way + b
             src[at] = (src[at].astype(F32) + merge[way, b].astype(F32)).astype(BF16)
         near(0, way).start()
-    design_grad(2, 0)
-    add_near(2)
-    to_y(2).start()
-    design_grad(2, 1)
     design_grad(3, 0)
     design_grad(3, 1)
     add_near(0)

time: 174 us -> 172 us (0.989); the launches traced: 174 us -> 170 us
  Pallas kernels: 173 us -> 169 us
    pallas_call x1, Pallas kernels: 170 us -> 166 us  [body(): pl.pallas_call(kernel, out_shape=(jax.ShapeDtypeStruct((1, ROWS), F32), j...]
where the time goes in v4:
time: 172 us; the launch traced here: 170 us
  Pallas kernels  169 us (98%)
    pallas_call x1, Pallas kernels, body(): pl.pallas_call(kernel, out_shape=(jax.ShapeDtypeStruct((1, ROWS), F32), j...  166 us

profile of v4, /device:TPU:9, one launch (start us, length us, event | category | flops | bytes accessed | tf_op | source)
XLA Modules:
  0.0 169.9 jit_solution(8179924357781571149)
XLA Ops:
  0.6 166.4 %shard_map.67 = (f32[1,1024]{1,0:T(1,128)}, bf16[1024,1024]{1,0:T(8,128)(2,1)}, f32[256,1024]{1,0:T(8,128)}) custom-call(bf16[1024,1024]{1,0:T(8,128)(2,1)} %des.1, f32[2048,1024]{1,0:T(8,128)} %proto.1, s32[1,24]{1,0:T(1,128)} %cand.1, s32[1,1024]{1,0:T(1,128)} %bitcast.2), custom_call_target="tpu_custom_call" | custom-call | tf_op jit(solution)/shard_map/pallas_call | solution.py:509
  167.0 2.8 %shard_map.68 = (f32[1,1024]{1,0:T(1,128)}, bf16[1024,1024]{1,0:T(8,128)(2,1)}, f32[256,1024]{1,0:T(8,128)}) custom-call(f32[1,1024]{1,0:T(1,128)} %get-tuple-element.9.losses, bf16[1024,1024]{1,0:T(8,128)(2,1)} %get-tuple-element.10.design_grad, f32[256,1024]{1,0:T(8,128)} %get-tuple-element.11.proto_grad), custom_call_target="tpu_custom_call" | custom-call | tf_op jit(solution)/shard_map/pallas_call | solution.py:589

commit v5 on v4

--- a/solution.py
+++ b/solution.py
@@ -58,7 +58,7 @@
     send, arr_m, arr_o, des_m, des_o, dt_m, dt_o, grads, stage, merge, from_up, from_down, from_y, far_y, runs, core_in, dg_s,
     prow, m_run, s_run, pick, total, req_v, req_in, order_v, req_own, req_s, order_s,
     ld_sem, des_sem, out_sem, loc_sem, own_sem, rq_s, rq_r, ag_s, ag_r, rl_s, rl_r, gy_s, gy_r, ha_s, ha_r, f_s, fm_r, fo_r, b_s, b_r,
-    fy_s, fy_r, mg_s, mg_r, rs_s, rs_r, y_s, y_r, c_s, c_r,
+    fy_s, fy_r, gv_s, gv_r, mg_s, mg_r, rs_s, rs_r, y_s, y_r, c_s, c_r,
 ):
     p, d = lax.axis_index("proto"), lax.axis_index("design")
     x, z, y, r = p // SIDE, p % SIDE, d // 2, d % 2
@@ -310,8 +310,6 @@
 
         mine = jnp.dot(grads[kv, ku], des_m[...], preferred_element_type=F32).astype(BF16).reshape(2, TILE, HALF)
         send[kv * 2, ku] = mine
-        other = jnp.dot(grads[kv, ku], des_o[...], preferred_element_type=F32).astype(BF16).reshape(2, TILE, HALF)
-        send[ku * 2 + 1, kv] = other
 
         @pl.when((ku == 0) & (kv == 0))
         def _():
@@ -326,6 +324,10 @@
             @pl.when((ku == k) & (kv != 0))
             def _():
                 back_mine(ku, kv, k).start()
+
+        other = jnp.dot(grads[kv, ku], des_o[...], preferred_element_type=F32).astype(BF16).reshape(2, TILE, HALF)
+        send[ku * 2 + 1, kv] = other
+        for k in (1, 2, 3):
 
             @pl.when(kv == k)
             def _():
@@ -375,10 +377,23 @@
         part = pl.ds(4 * y + 2 * way, 2)
         return remote(tab2.at[part], merge.at[way], mg_s.at[way], mg_r.at[way], along_u(1 if way == 0 else 3, r))
 
+    def given(way):
+        return from_y.at[0] if way == 0 else far_y.at[0]
+
+    def give(way, k):
+        low = 0 if k == 1 else 2
+        part = pl.ds(((y + k) % SIDE) * 4 + low, 2)
+        src = tab1 if way == 0 else tab3
+        return remote(src.at[part], given(way).at[pl.ds(low, 2)], gv_s.at[way, k // 2], gv_r.at[way, k // 2], along_y(k))
+
+    kept = ((0, 4), (2, 2), (0, 4), (0, 2))
+
     def near(k, way):
+        low, count = kept[k]
+        part, here = pl.ds(((y + k) % SIDE) * 4 + low, count), pl.ds(low, count)
         if way == 0:
-            return remote(tab1.at[group(k)], from_down.at[k], rs_s.at[0, k], rs_r.at[0, k], along_u(1, r))
-        return remote(tab3.at[group(k)], from_up.at[k], rs_s.at[1, k], rs_r.at[1, k], along_u(3, r))
+            return remote(tab1.at[part], from_down.at[k, here], rs_s.at[0, k], rs_r.at[0, k], along_u(1, r))
+        return remote(tab3.at[part], from_up.at[k, here], rs_s.at[1, k], rs_r.at[1, k], along_u(3, r))
 
     def to_y(k):
         return remote(tab0.at[group(k)], from_y.at[SIDE - k], y_s.at[k], y_r.at[SIDE - k], along_y(k))
@@ -392,10 +407,11 @@
     for kv in (1, 3, 2):
         back_mine(0, kv, 0).start()
     design_grad(0, 0)
-    sums(3)
-    near(2, 1).start()
-    sums(1)
-    near(2, 0).start()
+    for way, ku in ((1, 3), (0, 1)):
+        sums(ku)
+        give(way, 1).start()
+        give(way, 3).start()
+        near(2, way).start()
     for ku in (0, 1, 3, 2):
         back_other(ku, 0, 0).start()
     for k in (1, 3):
@@ -418,7 +434,8 @@
     def add_near(k):
         near(k, 0).wait_recv()
         near(k, 1).wait_recv()
-        for b in range(4):
+        low, count = kept[k]
+        for b in range(low, low + count):
             at = ((y + k) % SIDE) * 4 + b
             val = tab0[at].astype(F32) + from_up[k, b].astype(F32) + from_down[k, b].astype(F32)
             tab0[at] = val.astype(BF16)
@@ -433,10 +450,14 @@
     to_y(3).start()
     for way in (0, 1):
         src = tab1 if way == 0 else tab3
+        give(way, 1).wait_recv()
+        give(way, 3).wait_recv()
         far(way).wait_recv()
-        for b in range(2):
-            at = 4 * y + 2 * way + b
-            src[at] = (src[at].astype(F32) + merge[way, b].astype(F32)).astype(BF16)
+        for b in range(4):
+            val = src[4 * y + b].astype(F32) + given(way)[b].astype(F32)
+            if b // 2 == way:
+                val += merge[way, b % 2].astype(F32)
+            src[4 * y + b] = val.astype(BF16)
         near(0, way).start()
     design_grad(3, 0)
     design_grad(3, 1)
@@ -475,8 +496,10 @@
             to_y(k).wait_send()
         for h in range(2):
             dg_out(k, h).wait()
-    far(0).wait_send()
-    far(1).wait_send()
+    for way in (0, 1):
+        far(way).wait_send()
+        give(way, 1).wait_send()
+        give(way, 3).wait_send()
     cross.wait_send()
     for c in outs:
         c.wait()
@@ -573,6 +596,8 @@
             dma(4, 4, 2),
             dma(4),
             dma(4),
+            dma(2, 2),
+            dma(2, 2),
             dma(2),
             dma(2),
             dma(2, 4),

time: 172 us -> 178 us (1.035)
  the two profiles are of different devices: /device:TPU:9 before, /device:TPU:39 now
where the time goes in v5:
time: 178 us
  Pallas kernels  177 us (99%)
    pallas_call x1, Pallas kernels, body(): pl.pallas_call(kernel, out_shape=(jax.ShapeDtypeStruct((1, ROWS), F32), j...  174 us

profile of v5, /device:TPU:39, one launch (start us, length us, event | category | flops | bytes accessed | tf_op | source)
XLA Modules:
  0.0 177.9 jit_solution(3222523672776075804)
XLA Ops:
  0.6 174.5 %shard_map.67 = (f32[1,1024]{1,0:T(1,128)}, bf16[1024,1024]{1,0:T(8,128)(2,1)}, f32[256,1024]{1,0:T(8,128)}) custom-call(bf16[1024,1024]{1,0:T(8,128)(2,1)} %des.1, f32[2048,1024]{1,0:T(8,128)} %proto.1, s32[1,24]{1,0:T(1,128)} %cand.1, s32[1,1024]{1,0:T(1,128)} %bitcast.2), custom_call_target="tpu_custom_call" | custom-call | tf_op jit(solution)/shard_map/pallas_call | solution.py:532
  175.1 2.8 %shard_map.68 = (f32[1,1024]{1,0:T(1,128)}, bf16[1024,1024]{1,0:T(8,128)(2,1)}, f32[256,1024]{1,0:T(8,128)}) custom-call(f32[1,1024]{1,0:T(1,128)} %get-tuple-element.9.losses, bf16[1024,1024]{1,0:T(8,128)(2,1)} %get-tuple-element.10.design_grad, f32[256,1024]{1,0:T(8,128)} %get-tuple-element.11.proto_grad), custom_call_target="tpu_custom_call" | custom-call | tf_op jit(solution)/shard_map/pallas_call | solution.py:614

commit v6 on v4

--- a/solution.py
+++ b/solution.py
@@ -200,11 +200,11 @@
     for k in (3, 2):
         own_chunk(k, 0).start()
         own_chunk(k, 1).start()
+    wanted_blocks(0)
     for way in (0, 1):
         relay(way).wait_recv()
     for k in (1, 3, 2):
         share(k).start()
-    wanted_blocks(0)
     for way, ku in ((1, 1), (0, 3)):
         for k in (1, 2, 3):
             own_chunk(k, way).wait_recv()
@@ -391,13 +391,13 @@
     pl.loop(12, 16)(second_pass)
     for kv in (1, 3, 2):
         back_mine(0, kv, 0).start()
+    for ku in (0, 1, 3, 2):
+        back_other(ku, 0, 0).start()
     design_grad(0, 0)
     sums(3)
     near(2, 1).start()
     sums(1)
     near(2, 0).start()
-    for ku in (0, 1, 3, 2):
-        back_other(ku, 0, 0).start()
     for k in (1, 3):
         near(k, 1).start()
         near(k, 0).start()

time: 172 us -> 171 us (level)
  no operation moved by 1% of the time
where the time goes in v6:
time: 171 us; the launch traced here: 169 us
  Pallas kernels  169 us (99%)
    pallas_call x1, Pallas kernels, body(): pl.pallas_call(kernel, out_shape=(jax.ShapeDtypeStruct((1, ROWS), F32), j...  166 us

profile of v6, /device:TPU:9, one launch (start us, length us, event | category | flops | bytes accessed | tf_op | source)
XLA Modules:
  0.0 169.2 jit_solution(6338045361121037508)
XLA Ops:
  0.6 165.7 %shard_map.67 = (f32[1,1024]{1,0:T(1,128)}, bf16[1024,1024]{1,0:T(8,128)(2,1)}, f32[256,1024]{1,0:T(8,128)}) custom-call(bf16[1024,1024]{1,0:T(8,128)(2,1)} %des.1, f32[2048,1024]{1,0:T(8,128)} %proto.1, s32[1,24]{1,0:T(1,128)} %cand.1, s32[1,1024]{1,0:T(1,128)} %bitcast.2), custom_call_target="tpu_custom_call" | custom-call | tf_op jit(solution)/shard_map/pallas_call | solution.py:509
  166.3 2.8 %shard_map.68 = (f32[1,1024]{1,0:T(1,128)}, bf16[1024,1024]{1,0:T(8,128)(2,1)}, f32[256,1024]{1,0:T(8,128)}) custom-call(f32[1,1024]{1,0:T(1,128)} %get-tuple-element.9.losses, bf16[1024,1024]{1,0:T(8,128)(2,1)} %get-tuple-element.10.design_grad, f32[256,1024]{1,0:T(8,128)} %get-tuple-element.11.proto_grad), custom_call_target="tpu_custom_call" | custom-call | tf_op jit(solution)/shard_map/pallas_call | solution.py:589

commit v7 on v6

--- a/solution.py
+++ b/solution.py
@@ -169,8 +169,12 @@
                     arr_m[0, ku, i] = val
                 else:
                     send[n, ku, i] = val
-            if n:
+            if n not in (0, 4, 5):
                 fetched(n, ku).start()
+
+    def opposite(ku):
+        for n in (4, 5):
+            fetched(n, ku).start()
 
     def fetched(n, ku):
         k, so = n // 2, n % 2
@@ -211,9 +215,12 @@
         hand(way, 1).wait_recv()
         hand(way, 3).wait_recv()
         wanted_blocks(ku)
+        opposite(0 if ku == 1 else 1)
     for k in (1, 2, 3):
         remote(tab2.at[group(0)], tab2.at[group(0)], gy_s.at[k], gy_r.at[k], sibling).wait_recv()
     wanted_blocks(2)
+    opposite(3)
+    opposite(2)
 
     for ku in range(4):
         first = owner(ku, 0) * 2
@@ -310,8 +317,6 @@
 
         mine = jnp.dot(grads[kv, ku], des_m[...], preferred_element_type=F32).astype(BF16).reshape(2, TILE, HALF)
         send[kv * 2, ku] = mine
-        other = jnp.dot(grads[kv, ku], des_o[...], preferred_element_type=F32).astype(BF16).reshape(2, TILE, HALF)
-        send[ku * 2 + 1, kv] = other
 
         @pl.when((ku == 0) & (kv == 0))
         def _():
@@ -326,6 +331,10 @@
             @pl.when((ku == k) & (kv != 0))
             def _():
                 back_mine(ku, kv, k).start()
+
+        other = jnp.dot(grads[kv, ku], des_o[...], preferred_element_type=F32).astype(BF16).reshape(2, TILE, HALF)
+        send[ku * 2 + 1, kv] = other
+        for k in (1, 2, 3):
 
             @pl.when(kv == k)
             def _():
@@ -484,11 +493,11 @@
 
 def settle(losses, design_grad, proto_grad, losses_o, design_grad_o, proto_grad_o, one, many, few, sems):
     moves = [(losses, one, losses_o)]
+    for i in range(8):
+        part = pl.ds(i * TILE, TILE)
+        moves.append((design_grad.at[part], many.at[part], design_grad_o.at[part]))
     for i in range(4):
-        part = pl.ds(i * COLS, COLS)
-        moves.append((design_grad.at[part], many.at[part], design_grad_o.at[part]))
-    for i in range(2):
-        part = pl.ds(i * TILE, TILE)
+        part = pl.ds(i * 64, 64)
         moves.append((proto_grad.at[part], few.at[part], proto_grad_o.at[part]))
     reads = [pltpu.make_async_copy(a, b, sems.at[0, n]) for n, (a, b, c) in enumerate(moves)]
     writes = [pltpu.make_async_copy(b, c, sems.at[1, n]) for n, (a, b, c) in enumerate(moves)]
@@ -595,7 +604,7 @@
         ),
         in_specs=[pl.BlockSpec(memory_space=pl.ANY)] * 3,
         out_specs=(pl.BlockSpec(memory_space=pl.ANY),) * 3,
-        scratch_shapes=[vmem((1, ROWS), F32), vmem((ROWS, D), BF16), vmem((PAIR, D), F32), dma(2, 7)],
+        scratch_shapes=[vmem((1, ROWS), F32), vmem((ROWS, D), BF16), vmem((PAIR, D), F32), dma(2, 13)],
     )(losses, design_grad, proto_grad)
     return losses.reshape(ROWS), design_grad, proto_grad
 

time: 171 us -> 172 us (level)
  no operation moved by 1% of the time
where the time goes in v7:
time: 172 us; the launch traced here: 171 us
  Pallas kernels  170 us (99%)
    pallas_call x1, Pallas kernels, body(): pl.pallas_call(kernel, out_shape=(jax.ShapeDtypeStruct((1, ROWS), F32), j...  167 us

profile of v7, /device:TPU:9, one launch (start us, length us, event | category | flops | bytes accessed | tf_op | source)
XLA Modules:
  0.0 170.8 jit_solution(11686637207585761995)
XLA Ops:
  0.6 167.4 %shard_map.67 = (f32[1,1024]{1,0:T(1,128)}, bf16[1024,1024]{1,0:T(8,128)(2,1)}, f32[256,1024]{1,0:T(8,128)}) custom-call(bf16[1024,1024]{1,0:T(8,128)(2,1)} %des.1, f32[2048,1024]{1,0:T(8,128)} %proto.1, s32[1,24]{1,0:T(1,128)} %cand.1, s32[1,1024]{1,0:T(1,128)} %bitcast.2), custom_call_target="tpu_custom_call" | custom-call | tf_op jit(solution)/shard_map/pallas_call | solution.py:518
  168.0 2.8 %shard_map.68 = (f32[1,1024]{1,0:T(1,128)}, bf16[1024,1024]{1,0:T(8,128)(2,1)}, f32[256,1024]{1,0:T(8,128)}) custom-call(f32[1,1024]{1,0:T(1,128)} %get-tuple-element.9.losses, bf16[1024,1024]{1,0:T(8,128)(2,1)} %get-tuple-element.10.design_grad, f32[256,1024]{1,0:T(8,128)} %get-tuple-element.11.proto_grad), custom_call_target="tpu_custom_call" | custom-call | tf_op jit(solution)/shard_map/pallas_call | solution.py:598
